TPU v7x, 32 devices: a whole 2x2x4 slice. The times are simulated.
32 devices in a mesh: seq: 8 (over z, y), head: 4 (over x, core).
Axes of the slice: x: 2, y: 2, z: 4, core: 2. Of those that a mesh axis runs over, the one named last changes fastest.
Arguments:
- layer_input: bfloat16 [4, 1024, 8192], P('head', 'seq'), may hold values from -6 to 6
- out_grad: bfloat16 [4, 1024, 8192], P('head', 'seq'), may hold values from -6 to 6
- attention_out: bfloat16 [4, 1024, 4096], P('head', 'seq'), may hold values from -6 to 6
- frozen_output_grad: bfloat16 [4, 1024, 4096], P('head', 'seq'), may hold values from -6 to 6
- query_rows: bfloat16 [4, 1024, 4096], P('head', 'seq'), may hold values from -120 to 120
- key_rows: bfloat16 [4, 1024, 512], P('head', 'seq'), may hold values from -4 to 4
- value_rows: bfloat16 [4, 1024, 512], P('head', 'seq'), may hold values from -6 to 6
- seg_lengths: int32 [4, 8], P('head'), may hold values from 1 to 256, 1024 in all within a row
- use_list: int32 [4, 8], replicated, may hold values from 0 to 31, as said below
- store_map: int32 [32], replicated, may hold values from 0 to 31, as said below
- query_down: float32 [32, 64, 8192], P('head', None, 'seq'), may hold values from -0.0625 to 0.0625
- query_up: float32 [32, 64, 4096], P('head', None, 'seq'), may hold values from -0.75 to 0.75
- output_down: float32 [32, 64, 4096], P('head', None, 'seq'), may hold values from -0.09375 to 0.09375
- output_up: float32 [32, 64, 8192], P('head', None, 'seq'), may hold values from -0.75 to 0.75
Outputs:
- grad_query_down: float32 [32, 64, 8192], P('head', None, 'seq')
- grad_query_up: float32 [32, 64, 4096], P('head', None, 'seq')
- grad_output_down: float32 [32, 64, 4096], P('head', None, 'seq')
- grad_output_up: float32 [32, 64, 8192], P('head', None, 'seq')
Inputs may be any that keep to these rules, and one draw needn't show every extreme that they name: `use_list`: each row names 8 distinct tenants. Counting a tenant's store index as store_map[tenant] // 8, a row names at most 2 tenants of one store index, and exactly 2 of some store index in every row. A permutation: tenant t's adapters are in slot store_map[t]. `seg_lengths`: each row sums to 1024.
All inputs are finite; a program needn't handle non-finite values.
Results may differ from a plain program's by a relative error of at most 0.024.
Values may be sent and summed in bfloat16 or wider, within the bound.
A program may use at most 128 MiB of HBM per device.

v0:
```python
import math
import jax
import jax.numpy as jnp
from jax import lax
from jax.sharding import PartitionSpec as P

QH = 32
KVH = 4
HD = 128
CAP = 2
adapter_scale = 2.0
big_negative = -1e30
highest = lax.Precision.HIGHEST


def contract_axes(left_side, right_side, left_dim, right_dim):
    return lax.dot_general(
        left_side,
        right_side,
        (((left_dim,), (right_dim,)), ((), ())),
        preferred_element_type=jnp.float32,
    )


def narrow(full_rows, tenant_row_mask, rank_size):
    length, used_count = tenant_row_mask.shape
    return jnp.sum(
        full_rows.reshape(length, used_count, rank_size) * tenant_row_mask[:, :, None], axis=1
    )


def widened_rows(low_rows, tenant_row_mask):
    length, used_count = tenant_row_mask.shape
    spread_rows = tenant_row_mask.astype(jnp.bfloat16)[:, :, None] * low_rows[:, None, :]
    return spread_rows.reshape(length, used_count * low_rows.shape[1])


def request_tables(use_list, store_map, slots_dev):
    tenants = store_map.shape[0]
    used_count = use_list.shape[1]
    matches = use_list[:, :, None] == jnp.arange(tenants, dtype=jnp.int32)[None, None, :]
    slot_index = jnp.sum(jnp.where(matches, store_map[None, None, :], 0), axis=2)
    owner_index = slot_index // slots_dev
    local_slot = slot_index % slots_dev
    same_owner = (owner_index[:, :, None] == owner_index[:, None, :]).astype(jnp.int32)
    indices = jnp.arange(used_count, dtype=jnp.int32)
    earlier = (indices[None, :] < indices[:, None]).astype(jnp.int32)
    rank_index = jnp.sum(same_owner * earlier[None, :, :], axis=2)
    return (owner_index, local_slot, rank_index)


def attention_grad(query_heads, key_heads, value_heads, gradient_heads, segment, key_span):
    length, head_count, head_width = query_heads.shape
    block_rows = min(512, length)
    window = block_rows + key_span
    factor = 1.0 / math.sqrt(head_width)
    padded_keys = jnp.pad(key_heads, ((key_span, 0), (0, 0), (0, 0)))
    padded_values = jnp.pad(value_heads, ((key_span, 0), (0, 0), (0, 0)))
    padded_segment = jnp.concatenate([jnp.full((key_span,), -1, jnp.int32), segment])

    def one_block(row_start):
        query_block = lax.dynamic_slice_in_dim(query_heads, row_start, block_rows, 0)
        grad_block = lax.dynamic_slice_in_dim(gradient_heads, row_start, block_rows, 0)
        key_block = lax.dynamic_slice_in_dim(padded_keys, row_start, window, 0)
        value_block = lax.dynamic_slice_in_dim(padded_values, row_start, window, 0)
        query_segment = lax.dynamic_slice_in_dim(segment, row_start, block_rows, 0)
        key_segment = lax.dynamic_slice_in_dim(padded_segment, row_start, window, 0)
        query_pos = row_start + jnp.arange(block_rows, dtype=jnp.int32)
        key_pos = row_start - key_span + jnp.arange(window, dtype=jnp.int32)
        allowed = (query_segment[:, None] == key_segment[None, :]) & (
            key_pos[None, :] <= query_pos[:, None]
        )
        scores = (
            jnp.einsum("qhd,khd->hqk", query_block, key_block, preferred_element_type=jnp.float32)
            * factor
        )
        scores = jnp.where(allowed[None, :, :], scores, big_negative)
        row_max = jnp.max(scores, axis=2, keepdims=True)
        weights = jnp.exp(scores - row_max)
        probabilities = weights / jnp.sum(weights, axis=2, keepdims=True)
        prob_grad = jnp.einsum(
            "qhd,khd->hqk", grad_block, value_block, preferred_element_type=jnp.float32
        )
        inner = jnp.sum(probabilities * prob_grad, axis=2, keepdims=True)
        score_grad = (probabilities * (prob_grad - inner)).astype(jnp.bfloat16)
        query_gradient = (
            jnp.einsum("hqk,khd->qhd", score_grad, key_block, preferred_element_type=jnp.float32)
            * factor
        )
        return query_gradient.astype(jnp.bfloat16)

    starts = jnp.arange(0, length, block_rows, dtype=jnp.int32)
    return lax.map(one_block, starts).reshape(length, head_count * head_width)


def shards(
    layer_input,
    out_grad,
    attention_out,
    frozen_output_grad,
    query_rows,
    key_rows,
    value_rows,
    seg_lengths,
    use_list,
    store_map,
    query_down,
    query_up,
    output_down,
    output_up,
):
    slots_dev = query_down.shape[0]
    rank_size = query_down.shape[1]
    group_size = QH // KVH
    input_columns, gradient_columns, head_outputs, base_heads, query_heads = (
        lax.all_to_all(layer_input[0], "seq", split_axis=1, concat_axis=0, tiled=True),
        lax.all_to_all(out_grad[0], "seq", split_axis=1, concat_axis=0, tiled=True),
        lax.all_to_all(attention_out[0], "seq", split_axis=1, concat_axis=0, tiled=True),
        lax.all_to_all(frozen_output_grad[0], "seq", split_axis=1, concat_axis=0, tiled=True),
        lax.all_to_all(query_rows[0], "seq", split_axis=1, concat_axis=0, tiled=True),
    )
    length = input_columns.shape[0]
    heads_here = query_heads.shape[1] // HD
    first_head = lax.axis_index("seq") * heads_here
    gathered_keys, gathered_values = (
        lax.all_gather(key_rows[0], "seq", axis=0, tiled=True),
        lax.all_gather(value_rows[0], "seq", axis=0, tiled=True),
    )
    kv_index = (first_head + jnp.arange(heads_here, dtype=jnp.int32)) // group_size
    key_heads = jnp.take(gathered_keys.reshape(length, KVH, HD), kv_index, axis=1)
    value_heads = jnp.take(gathered_values.reshape(length, KVH, HD), kv_index, axis=1)
    owner_index, local_slot, rank_index = request_tables(use_list, store_map, slots_dev)
    my_index = lax.axis_index("head")
    batch_count = use_list.shape[0]
    cap_ids = jnp.arange(CAP, dtype=jnp.int32)
    slot_ids = jnp.arange(slots_dev, dtype=jnp.int32)
    matched = (
        (owner_index == my_index)[:, :, None, None]
        & (rank_index[:, :, None, None] == cap_ids[None, None, :, None])
        & (local_slot[:, :, None, None] == slot_ids[None, None, None, :])
    )
    select = jnp.sum(matched.astype(jnp.float32), axis=1)

    def pack_slots(store_part):
        return jnp.einsum("mcl,lrw->mcrw", select, store_part, precision=highest).astype(
            jnp.bfloat16
        )

    fetched = (
        lax.all_to_all(pack_slots(query_down), "head", split_axis=0, concat_axis=0, tiled=True),
        lax.all_to_all(pack_slots(query_up), "head", split_axis=0, concat_axis=0, tiled=True),
        lax.all_to_all(pack_slots(output_down), "head", split_axis=0, concat_axis=0, tiled=True),
        lax.all_to_all(pack_slots(output_up), "head", split_axis=0, concat_axis=0, tiled=True),
    )
    mine_owner = lax.dynamic_index_in_dim(owner_index, my_index, 0, keepdims=False)
    mine_rank = lax.dynamic_index_in_dim(rank_index, my_index, 0, keepdims=False)
    store_ids = jnp.arange(batch_count, dtype=jnp.int32)
    picker = (
        (mine_owner[:, None, None] == store_ids[None, :, None])
        & (mine_rank[:, None, None] == cap_ids[None, None, :])
    ).astype(jnp.float32)
    picker_half = picker.astype(jnp.bfloat16)

    def unpack(received):
        chosen = jnp.einsum(
            "ijc,jcrw->irw", picker_half, received, preferred_element_type=jnp.float32
        ).astype(jnp.bfloat16)
        return chosen.reshape(chosen.shape[0] * chosen.shape[1], chosen.shape[2])

    flattened_list = [unpack(received) for received in fetched]
    lengths = seg_lengths[0]
    used_count = lengths.shape[0]
    offsets = jnp.cumsum(lengths) - lengths
    positions = jnp.arange(length, dtype=jnp.int32)
    segment = jnp.sum((positions[:, None] >= offsets[None, :]).astype(jnp.int32), axis=1) - 1
    tenant_row_mask = (segment[:, None] == jnp.arange(used_count, dtype=jnp.int32)[None, :]).astype(
        jnp.float32
    )
    partial_out = narrow(
        contract_axes(head_outputs, flattened_list[2], 1, 1), tenant_row_mask, rank_size
    )
    partial_grad = narrow(
        contract_axes(gradient_columns, flattened_list[3], 1, 1), tenant_row_mask, rank_size
    )
    partial_query = narrow(
        contract_axes(input_columns, flattened_list[0], 1, 1), tenant_row_mask, rank_size
    )
    summed_out, summed_grad, summed_query = (
        lax.psum(partial_out.astype(jnp.bfloat16), "seq").astype(jnp.float32),
        lax.psum(partial_grad.astype(jnp.bfloat16), "seq").astype(jnp.float32),
        lax.psum(partial_query.astype(jnp.bfloat16), "seq").astype(jnp.float32),
    )
    low_rank_output = summed_out.astype(jnp.bfloat16)
    low_grad = summed_grad.astype(jnp.bfloat16)
    low_rank_query = summed_query.astype(jnp.bfloat16)
    widened_gradient = widened_rows(low_grad, tenant_row_mask)
    gradient_heads = (
        base_heads.astype(jnp.float32)
        + adapter_scale
        * jnp.dot(widened_gradient, flattened_list[2], preferred_element_type=jnp.float32)
    ).astype(jnp.bfloat16)
    query_gradient = attention_grad(
        query_heads.reshape(length, heads_here, HD),
        key_heads,
        value_heads,
        gradient_heads.reshape(length, heads_here, HD),
        segment,
        length // 4,
    )
    partial_back = narrow(
        contract_axes(query_gradient, flattened_list[1], 1, 1), tenant_row_mask, rank_size
    )
    low_rank_back = lax.psum(partial_back.astype(jnp.bfloat16), "seq")
    outer_products = (
        adapter_scale
        * contract_axes(widened_rows(low_rank_back, tenant_row_mask), input_columns, 0, 0),
        adapter_scale
        * contract_axes(widened_rows(low_rank_query, tenant_row_mask), query_gradient, 0, 0),
        adapter_scale * contract_axes(widened_gradient, head_outputs, 0, 0),
        adapter_scale
        * contract_axes(widened_rows(low_rank_output, tenant_row_mask), gradient_columns, 0, 0),
    )

    def spread(gradient):
        pieces = gradient.reshape(used_count, rank_size, gradient.shape[1])
        return jnp.einsum("ijc,irw->jcrw", picker, pieces, precision=highest)

    returned = (
        lax.all_to_all(
            spread(outer_products[0]).astype(jnp.bfloat16),
            "head",
            split_axis=0,
            concat_axis=0,
            tiled=True,
        ).astype(jnp.float32),
        lax.all_to_all(
            spread(outer_products[1]).astype(jnp.bfloat16),
            "head",
            split_axis=0,
            concat_axis=0,
            tiled=True,
        ).astype(jnp.float32),
        lax.all_to_all(
            spread(outer_products[2]).astype(jnp.bfloat16),
            "head",
            split_axis=0,
            concat_axis=0,
            tiled=True,
        ).astype(jnp.float32),
        lax.all_to_all(
            spread(outer_products[3]).astype(jnp.bfloat16),
            "head",
            split_axis=0,
            concat_axis=0,
            tiled=True,
        ).astype(jnp.float32),
    )

    def settle(received):
        return jnp.einsum("mcl,mcrw->lrw", select, received, precision=highest)

    return (settle(returned[0]), settle(returned[1]), settle(returned[2]), settle(returned[3]))


def solution(mesh):
    placed = (
        P("head", "seq", None),
        P("head", "seq", None),
        P("head", "seq", None),
        P("head", "seq", None),
        P("head", "seq", None),
        P("head", "seq", None),
        P("head", "seq", None),
        P("head", None),
        P(),
        P(),
        P("head", None, "seq"),
        P("head", None, "seq"),
        P("head", None, "seq"),
        P("head", None, "seq"),
    )
    return jax.shard_map(
        shards,
        mesh=mesh,
        in_specs=placed,
        out_specs=(
            P("head", None, "seq"),
            P("head", None, "seq"),
            P("head", None, "seq"),
            P("head", None, "seq"),
        ),
        check_vma=False,
    )
```

profile of v0, /device:TPU:0, one launch (start us, length us, event | category | flops | bytes accessed | tf_op | source)
XLA Modules:
  0.0 579.0 jit_solution(9823844953946376288)
XLA Ops:
  13.1 4.2 all-to-all-start.4
  20.1 6.7 %all-to-all-done.4 = bf16[4,2,64,512]{3,1,2,0:T(2,128)(2,1)} async-done(((bf16[4,2,64,512]{3,1,2,0:T(2,128)(2,1)}), bf16[4,2,64,512]{3,1,2,0:T(2,128)(2,1)}, u32[]{:S(2)}, u32[]{:S(2)}) %all-to-all-start.4) | async-done | bytes 524320 | tf_op jit(solution)/shard_map/all_to_all | solution.py:152
  43.5 5.4 fusion.34
  50.7 7.2 %all-to-all-done.2 = bf16[4,2,64,1024]{3,1,2,0:T(2,128)(2,1)S(1)} async-done(((bf16[4,2,64,1024]{3,1,2,0:T(2,128)(2,1)}), bf16[4,2,64,1024]{3,1,2,0:T(2,128)(2,1)S(1)}, u32[]{:S(2)}, u32[]{:S(2)}) %all-to-all-start.2) | async-done | bytes 1048608 | tf_op jit(solution)/shard_map/all_to_all | solution.py:153
  63.8 13.1 %all-to-all-done.8 = bf16[4,2,64,1024]{3,1,2,0:T(2,128)(2,1)S(1)} async-done(((bf16[4,2,64,1024]{3,1,2,0:T(2,128)(2,1)}), bf16[4,2,64,1024]{3,1,2,0:T(2,128)(2,1)S(1)}, u32[]{:S(2)}, u32[]{:S(2)}) %all-to-all-start.8) | async-done | bytes 1048608 | tf_op jit(solution)/shard_map/all_to_all | solution.py:150
  77.8 6.7 %all-to-all-start.10 = ((bf16[128,8,512]{0,2,1:T(8,128)(2,1)}), bf16[128,8,512]{0,2,1:T(8,128)(2,1)S(1)}, u32[]{:S(2)}, u32[]{:S(2)}) async-start(bf16[128,8,512]{0,2,1:T(8,128)(2,1)} %bitcast.60), calls=%async_computation.10 | async-start | bytes 2097152 | tf_op jit(solution)/shard_map/all_to_all | solution.py:118
  85.8 24.3 %all-to-all-done.10 = bf16[128,8,512]{0,2,1:T(8,128)(2,1)S(1)} async-done(((bf16[128,8,512]{0,2,1:T(8,128)(2,1)}), bf16[128,8,512]{0,2,1:T(8,128)(2,1)S(1)}, u32[]{:S(2)}, u32[]{:S(2)}) %all-to-all-start.10) | async-done | bytes 1048608 | tf_op jit(solution)/shard_map/all_to_all | solution.py:118
  117.8 21.8 %all-to-all-done = bf16[128,8,512]{0,2,1:T(8,128)(2,1)S(1)} async-done(((bf16[128,8,512]{0,2,1:T(8,128)(2,1)}), bf16[128,8,512]{0,2,1:T(8,128)(2,1)S(1)}, u32[]{:S(2)}, u32[]{:S(2)}) %all-to-all-start) | async-done | bytes 1048608 | tf_op jit(solution)/shard_map/all_to_all | solution.py:120
  149.1 52.8 %all-to-all-done.3 = bf16[128,8,1024]{0,2,1:T(8,128)(2,1)S(1)} async-done(((bf16[128,8,1024]{0,2,1:T(8,128)(2,1)}), bf16[128,8,1024]{0,2,1:T(8,128)(2,1)S(1)}, u32[]{:S(2)}, u32[]{:S(2)}) %all-to-all-start.3) | async-done | bytes 2097184 | tf_op jit(solution)/shard_map/all_to_all | solution.py:117
  203.2 4.4 all-to-all-start.6
  217.7 47.6 %all-to-all-done.6 = bf16[128,8,1024]{0,2,1:T(8,128)(2,1)} async-done(((bf16[128,8,1024]{0,2,1:T(8,128)(2,1)}), bf16[128,8,1024]{0,2,1:T(8,128)(2,1)}, u32[]{:S(2)}, u32[]{:S(2)}) %all-to-all-start.6) | async-done | bytes 2097184 | tf_op jit(solution)/shard_map/all_to_all | solution.py:116
  265.3 4.5 all-to-all-start.1
  303.0 65.1 %all-reduce.7.cloned.1.call-done = bf16[1024,64]{0,1:T(8,128)(2,1)} async-done(((bf16[1024,64]{0,1:T(8,128)(2,1)}), bf16[1024,64]{0,1:T(8,128)(2,1)}) %all-reduce.7.cloned.1.call-update) | async-done | bytes 131088 | tf_op jit(solution)/shard_map/psum | solution.py:190
  371.1 50.4 %while.12 = (s32[]{:T(128)}, bf16[2,512,4,128]{3,2,1,0:T(4,128)(2,1)}, s32[2]{0:T(128)S(1)}, bf16[1280,4,128]{2,0,1:T(8,128)(2,1)S(1)}, s32[1024]{0:T(1024)S(1)}...) while((s32[]{:T(128)}, ...), condition=%wide.region_11.13_spmd, body=%wide.region_7.12_spmd.sunk | while | flops 1230110720 | bytes 50923260 | solution.py:93
  375.2 5.1 fusion.110
  382.2 7.7 %fusion.111 = (f32[4,512]{1,0:T(4,128)S(1)}, f32[4,512,768]{2,1,0:T(8,128)S(1)}) fusion(f32[4,512,768]{2,1,0:T(8,128)} %fusion.110, pred[512,768]{1,0:T(8,128)(4,1)S(1)} %compare_and_fusion.4), kind=kOutput, calls=%fused_computation.141.clone.1 | output fusion | flops 9437951 | bytes 12984320 | tf_op jit(solution)/shard_map/while/body/eval_jaxpr/sub | solution.py:79
  400.4 5.0 fusion.110
  407.3 7.7 %fusion.111 = (f32[4,512]{1,0:T(4,128)S(1)}, f32[4,512,768]{2,1,0:T(8,128)S(1)}) fusion(f32[4,512,768]{2,1,0:T(8,128)} %fusion.110, pred[512,768]{1,0:T(8,128)(4,1)S(1)} %compare_and_fusion.4), kind=kOutput, calls=%fused_computation.141.clone.1 | output fusion | flops 9437951 | bytes 12984320 | tf_op jit(solution)/shard_map/while/body/eval_jaxpr/sub | solution.py:79
  424.5 71.3 %all-reduce.9.cloned.1.call-done = (bf16[1024,64]{0,1:T(8,128)(2,1)}, bf16[1024,64]{0,1:T(8,128)(2,1)}, bf16[1024,64]{0,1:T(8,128)(2,1)}) async-done(((bf16[1024,64]{0,1:T(8,128)(2,1)}, bf16[1024,64]{0,1:T(8,128)(2,1)}, bf16[1024,64]{0,1:T(8,128)(2,1)}), (bf16[1024,64]{0,1:T(8,128)(2,1)}, bf16[1024,64]{0,1:T(8,128)(2,1)}, bf16[1024,64]{0,1:T(8,128)(2,1)})) %all-reduce.9.cloned.1.call-update) | async-done | bytes 393232 | tf_op jit(solution)/shard_map/psum | solution.py:213
  502.0 4.3 all-to-all-start.9
  510.9 4.3 all-to-all-done.9
  538.8 7.4 %all-to-all-done.12 = bf16[4,2,64,1024]{3,1,2,0:T(2,128)(2,1)S(1)} async-done(((bf16[4,2,64,1024]{3,1,2,0:T(2,128)(2,1)}), bf16[4,2,64,1024]{3,1,2,0:T(2,128)(2,1)S(1)}, u32[]{:S(2)}, u32[]{:S(2)}) %all-to-all-start.12) | async-done | bytes 1048608 | tf_op jit(solution)/shard_map/all_to_all | solution.py:250
  546.2 4.5 all-to-all-start.7
  565.2 4.3 convolution_bitcast_fusion.1
  (183 shorter events, 170.5 us)
Async XLA Ops:
  7.2 23.0 %copy-start = (f32[8,64,1024]{2,1,0:T(8,128)S(1)}, f32[8,64,1024]{2,1,0:T(8,128)}, u32[]{:S(2)}) copy-start(f32[8,64,1024]{2,1,0:T(8,128)} %param.31) | copy-start | bytes 6291460
  8.7 34.8 %copy-start.26 = (f32[4,2,8]{2,1,0:T(2,128)}, f32[4,2,8]{2,1,0:T(2,128)S(1)}, u32[]{:S(2)}) copy-start(f32[4,2,8]{2,1,0:T(2,128)S(1)} %convert_reduce_fusion.1) | copy-start | bytes 772
  13.1 13.7 %all-to-all-start.4 = ((bf16[4,2,64,512]{3,1,2,0:T(2,128)(2,1)}), bf16[4,2,64,512]{3,1,2,0:T(2,128)(2,1)}, u32[]{:S(2)}, u32[]{:S(2)}) async-start(bf16[4,2,64,512]{3,1,2,0:T(2,128)(2,1)} %copy.141), calls=%async_computation.4 | async-start | bytes 1048576 | tf_op jit(solution)/shard_map/all_to_all | solution.py:152
  26.7 12.3 %all-to-all-start.5 = ((bf16[4,2,64,512]{3,2,1,0:T(8,128)(2,1)}), bf16[4,2,64,512]{3,2,1,0:T(8,128)(2,1)S(1)}, u32[]{:S(2)}, u32[]{:S(2)}) async-start(bf16[4,2,64,512]{3,2,1,0:T(8,128)(2,1)} %copy.151), calls=%async_computation.5 | async-start | bytes 1048576 | tf_op jit(solution)/shard_map/all_to_all | solution.py:151
  39.8 18.1 %all-to-all-start.2 = ((bf16[4,2,64,1024]{3,1,2,0:T(2,128)(2,1)}), bf16[4,2,64,1024]{3,1,2,0:T(2,128)(2,1)S(1)}, u32[]{:S(2)}, u32[]{:S(2)}) async-start(bf16[4,2,64,1024]{3,1,2,0:T(2,128)(2,1)} %copy.134), calls=%async_computation.2 | async-start | bytes 2097152 | tf_op jit(solution)/shard_map/all_to_all | solution.py:153
  58.9 18.0 %all-to-all-start.8 = ((bf16[4,2,64,1024]{3,1,2,0:T(2,128)(2,1)}), bf16[4,2,64,1024]{3,1,2,0:T(2,128)(2,1)S(1)}, u32[]{:S(2)}, u32[]{:S(2)}) async-start(bf16[4,2,64,1024]{3,1,2,0:T(2,128)(2,1)} %copy.162), calls=%async_computation.8 | async-start | bytes 2097152 | tf_op jit(solution)/shard_map/all_to_all | solution.py:150
  62.5 22.1 %copy-start.11 = (bf16[1,128,4096]{2,1,0:T(8,128)(2,1)S(1)}, bf16[1,128,4096]{2,1,0:T(8,128)(2,1)}, u32[]{:S(2)}) copy-start(bf16[1,128,4096]{2,1,0:T(8,128)(2,1)} %param.22) | copy-start | bytes 3145732
  77.8 32.3 %all-to-all-start.10 = ((bf16[128,8,512]{0,2,1:T(8,128)(2,1)}), bf16[128,8,512]{0,2,1:T(8,128)(2,1)S(1)}, u32[]{:S(2)}, u32[]{:S(2)}) async-start(bf16[128,8,512]{0,2,1:T(8,128)(2,1)} %bitcast.60), calls=%async_computation.10 | async-start | bytes 2097152 | tf_op jit(solution)/shard_map/all_to_all | solution.py:118
  110.2 29.4 %all-to-all-start = ((bf16[128,8,512]{0,2,1:T(8,128)(2,1)}), bf16[128,8,512]{0,2,1:T(8,128)(2,1)S(1)}, u32[]{:S(2)}, u32[]{:S(2)}) async-start(bf16[128,8,512]{0,2,1:T(8,128)(2,1)} %bitcast.10), calls=%async_computation | async-start | bytes 2097152 | tf_op jit(solution)/shard_map/all_to_all | solution.py:120
  140.6 61.3 %all-to-all-start.3 = ((bf16[128,8,1024]{0,2,1:T(8,128)(2,1)}), bf16[128,8,1024]{0,2,1:T(8,128)(2,1)S(1)}, u32[]{:S(2)}, u32[]{:S(2)}) async-start(bf16[128,8,1024]{0,2,1:T(8,128)(2,1)} %bitcast.184), calls=%async_computation.3 | async-start | bytes 4194304 | tf_op jit(solution)/shard_map/all_to_all | solution.py:117
  144.2 131.8 %all-gather.5.cloned.1.call-start = ((), (), s32[]{:S(2)}) async-start(), calls=%async_computation.14 | async-start | bytes 1179648 | tf_op jit(solution)/shard_map/all_gather | solution.py:126
  203.2 62.1 %all-to-all-start.6 = ((bf16[128,8,1024]{0,2,1:T(8,128)(2,1)}), bf16[128,8,1024]{0,2,1:T(8,128)(2,1)}, u32[]{:S(2)}, u32[]{:S(2)}) async-start(bf16[128,8,1024]{0,2,1:T(8,128)(2,1)} %bitcast.183), calls=%async_computation.6 | async-start | bytes 4194304 | tf_op jit(solution)/shard_map/all_to_all | solution.py:116
  207.6 70.1 %all-gather.7.cloned.1.call-start = ((), (), s32[]{:S(2)}) async-start(), calls=%async_computation.15 | async-start | bytes 1179648 | tf_op jit(solution)/shard_map/all_gather | solution.py:127
  215.5 54.8 %copy-start.14 = (bf16[4,2,64,1024]{3,1,2,0:T(2,128)(2,1)S(1)}, bf16[4,2,64,1024]{3,1,2,0:T(2,128)(2,1)}, u32[]{:S(2)}) copy-start(bf16[4,2,64,1024]{3,1,2,0:T(2,128)(2,1)} %copy-done.13) | copy-start | bytes 3145732
  265.3 37.7 %all-to-all-start.1 = ((bf16[128,8,512]{0,2,1:T(8,128)(2,1)}), bf16[128,8,512]{0,2,1:T(8,128)(2,1)}, u32[]{:S(2)}, u32[]{:S(2)}) async-start(bf16[128,8,512]{0,2,1:T(8,128)(2,1)} %bitcast.12), calls=%async_computation.1 | async-start | bytes 2097152 | tf_op jit(solution)/shard_map/all_to_all | solution.py:119
  269.9 98.3 %all-reduce.7.cloned.1.call-start = ((), (), s32[]{:S(2)}) async-start(), calls=%async_computation.13 | async-start | bytes 262144 | tf_op jit(solution)/shard_map/psum | solution.py:190
  297.9 197.9 %all-reduce.9.cloned.1.call-start = ((), (), s32[]{:S(2)}) async-start(), calls=%async_computation.16 | async-start | bytes 786432 | tf_op jit(solution)/shard_map/psum | solution.py:213
  300.9 67.2 %copy-start.22 = (bf16[8,64,512]{2,0,1:T(8,128)(2,1)S(1)}, bf16[8,64,512]{2,0,1:T(8,128)(2,1)}, u32[]{:S(2)}) copy-start(bf16[8,64,512]{2,0,1:T(8,128)(2,1)} %copy-done.21) | copy-start | bytes 1572868
  423.0 72.8 %copy-start.23 = (bf16[1024,64]{0,1:T(8,128)(2,1)S(1)}, bf16[1024,64]{0,1:T(8,128)(2,1)}, u32[]{:S(2)}) copy-start(bf16[1024,64]{0,1:T(8,128)(2,1)} %all-reduce.7.cloned.1.call-done) | copy-start | bytes 393220
  502.0 13.2 %all-to-all-start.9 = ((bf16[4,2,64,512]{3,1,2,0:T(2,128)(2,1)}), bf16[4,2,64,512]{3,1,2,0:T(2,128)(2,1)}, u32[]{:S(2)}, u32[]{:S(2)}) async-start(bf16[4,2,64,512]{3,1,2,0:T(2,128)(2,1)} %copy.166), calls=%async_computation.9 | async-start | bytes 1048576 | tf_op jit(solution)/shard_map/all_to_all | solution.py:236
  515.2 13.0 %all-to-all-start.11 = ((bf16[4,2,64,512]{3,1,2,0:T(2,128)(2,1)}), bf16[4,2,64,512]{3,1,2,0:T(2,128)(2,1)}, u32[]{:S(2)}, u32[]{:S(2)}) async-start(bf16[4,2,64,512]{3,1,2,0:T(2,128)(2,1)} %copy.172), calls=%async_computation.11 | async-start | bytes 1048576 | tf_op jit(solution)/shard_map/all_to_all | solution.py:243
  528.3 18.0 %all-to-all-start.12 = ((bf16[4,2,64,1024]{3,1,2,0:T(2,128)(2,1)}), bf16[4,2,64,1024]{3,1,2,0:T(2,128)(2,1)S(1)}, u32[]{:S(2)}, u32[]{:S(2)}) async-start(bf16[4,2,64,1024]{3,1,2,0:T(2,128)(2,1)} %copy.177), calls=%async_computation.12 | async-start | bytes 2097152 | tf_op jit(solution)/shard_map/all_to_all | solution.py:250
  537.1 13.7 %copy-start.27 = (f32[4,2,8]{2,1,0:T(2,128)S(1)}, f32[4,2,8]{2,1,0:T(2,128)}, u32[]{:S(2)}) copy-start(f32[4,2,8]{2,1,0:T(2,128)} %copy-done.26) | copy-start | bytes 772
  546.2 19.0 %all-to-all-start.7 = ((bf16[4,2,64,1024]{3,1,2,0:T(2,128)(2,1)}), bf16[4,2,64,1024]{3,1,2,0:T(2,128)(2,1)}, u32[]{:S(2)}, u32[]{:S(2)}) async-start(bf16[4,2,64,1024]{3,1,2,0:T(2,128)(2,1)} %copy.157), calls=%async_computation.7 | async-start | bytes 2097152 | tf_op jit(solution)/shard_map/all_to_all | solution.py:229
  (23 other events, 106.6 us)
Sparse Core Ops, SparseCore 0:
  147.1 61.6 all-gather.4
  210.9 61.0 all-gather.6
  298.0 70.0 all-reduce.6
  424.6 71.1 all-reduce.8
where the time goes:
time: 588 us; the launch traced here: 579 us
  waiting for transfers between devices  329 us (56%)
  matrix products  79.1 us (13%)
  local copies, waits for them, and re-layouts  67.7 us (12%)
  starting transfers between devices  54.7 us (9%)
  other arithmetic  25.2 us (4%)
  between operations  14.8 us (3%)
  loops' own time  8.21 us (1%)
    psum x1, waiting for transfers between devices, shards(): low_rank_back = lax.psum(partial_back.astype(jnp.bfloat16), 'seq')  71.3 us
    psum x1, waiting for transfers between devices, shards(): lax.psum(partial_grad.astype(jnp.bfloat16), 'seq').astype(jnp.float32)  65.1 us
    all_to_all x1, waiting for transfers between devices, shards(): lax.all_to_all(out_grad[0], 'seq', split_axis=1, concat_axis=0, tiled=True)  52.8 us
    all_to_all x1, waiting for transfers between devices, shards(): lax.all_to_all(layer_input[0], 'seq', split_axis=1, concat_axis=0, tiled=...  47.6 us
    unnamed x71, local copies, waits for them, and re-layouts  28.1 us
    all_to_all x1, waiting for transfers between devices, shards(): lax.all_to_all(attention_out[0], 'seq', split_axis=1, concat_axis=0, tile...  24.3 us
    all_to_all x1, waiting for transfers between devices, shards(): lax.all_to_all(query_rows[0], 'seq', split_axis=1, concat_axis=0, tiled=T...  21.8 us
    sub x2, other arithmetic, one_block(): weights = jnp.exp(scores - row_max)  15.4 us
  transfers between devices with their start and end apart: 17, of which 14 were waited for; matrix products, arithmetic and copies ran while one was open for 17% of the time, Pallas kernels for 0%

commit v1 on v0

--- a/solution.py
+++ b/solution.py
@@ -11,6 +11,12 @@
 adapter_scale = 2.0
 big_negative = -1e30
 highest = lax.Precision.HIGHEST
+
+
+def summed_here(shard, axis):
+    blocks = lax.all_gather(shard, axis, axis=0, tiled=False)
+    total = blocks.sum(axis=0)
+    return total
 
 
 def contract_axes(left_side, right_side, left_dim, right_dim):
@@ -187,7 +193,7 @@
     )
     summed_out, summed_grad, summed_query = (
         lax.psum(partial_out.astype(jnp.bfloat16), "seq").astype(jnp.float32),
-        lax.psum(partial_grad.astype(jnp.bfloat16), "seq").astype(jnp.float32),
+        summed_here(partial_grad.astype(jnp.bfloat16), "seq").astype(jnp.float32),
         lax.psum(partial_query.astype(jnp.bfloat16), "seq").astype(jnp.float32),
     )
     low_rank_output = summed_out.astype(jnp.bfloat16)

time: 588 us -> 529 us (0.90)
  waiting for transfers between devices: 329 us -> 273 us
    psum x1 -> x0, waiting for transfers between devices: 65.1 us -> none  [shards(): lax.psum(partial_grad.astype(jnp.bfloat16), 'seq').astype(jnp.float32)]
    all_gather x0 -> x1, waiting for transfers between devices: none -> 27.9 us  [summed_here(): blocks = lax.all_gather(shard, axis, axis=0, tiled=False)]
    all_to_all x1, waiting for transfers between devices: 21.8 us -> 3.64 us  [shards(): lax.all_to_all(query_rows[0], 'seq', split_axis=1, concat_axis=0, tiled=T...]
    unnamed x71 -> x72, local copies, waits for them, and re-layouts: 28.1 us -> 26.2 us
  transfers between devices with their start and end apart: 17 -> 17, of which waited for: 14 -> 14; matrix products, arithmetic and copies ran while one was open for 17% -> 19% of each run, Pallas kernels for 0% -> 0%
where the time goes in v1:
time: 529 us; the launch traced here: 520 us
  waiting for transfers between devices  273 us (52%)
  matrix products  79 us (15%)
  local copies, waits for them, and re-layouts  65.8 us (12%)
  starting transfers between devices  55.7 us (11%)
  other arithmetic  24.3 us (5%)
  between operations  14.7 us (3%)
  loops' own time  7.5 us (1%)
    psum x1, waiting for transfers between devices, shards(): low_rank_back = lax.psum(partial_back.astype(jnp.bfloat16), 'seq')  70.4 us
    all_to_all x1, waiting for transfers between devices, shards(): lax.all_to_all(out_grad[0], 'seq', split_axis=1, concat_axis=0, tiled=True)  52.7 us
    all_to_all x1, waiting for transfers between devices, shards(): lax.all_to_all(layer_input[0], 'seq', split_axis=1, concat_axis=0, tiled=...  49 us
    all_gather x1, waiting for transfers between devices, summed_here(): blocks = lax.all_gather(shard, axis, axis=0, tiled=False)  27.9 us
    unnamed x72, local copies, waits for them, and re-layouts  26.2 us
    all_to_all x1, waiting for transfers between devices, shards(): lax.all_to_all(attention_out[0], 'seq', split_axis=1, concat_axis=0, tile...  23.2 us
    sub x2, other arithmetic, one_block(): weights = jnp.exp(scores - row_max)  15.1 us
    dot_general x8, matrix products, contract_axes(): lax.dot_general(left_side, right_side, (((left_dim,), (right_dim,)), ((),...  14.3 us
  transfers between devices with their start and end apart: 17, of which 14 were waited for; matrix products, arithmetic and copies ran while one was open for 19% of the time, Pallas kernels for 0%

profile of v1, /device:TPU:0, one launch (start us, length us, event | category | flops | bytes accessed | tf_op | source)
XLA Modules:
  0.0 520.0 jit_solution(18015893713077555286)
XLA Ops:
  13.1 4.2 all-to-all-start.4
  20.1 6.7 %all-to-all-done.4 = bf16[4,2,64,512]{3,1,2,0:T(2,128)(2,1)} async-done(((bf16[4,2,64,512]{3,1,2,0:T(2,128)(2,1)}), bf16[4,2,64,512]{3,1,2,0:T(2,128)(2,1)}, u32[]{:S(2)}, u32[]{:S(2)}) %all-to-all-start.4) | async-done | bytes 524320 | tf_op jit(solution)/shard_map/all_to_all | solution.py:158
  43.0 5.4 %fusion.34 = bf16[4,2,64,1024]{3,0,1,2:T(4,128)(2,1)S(1)} fusion(f32[8,64,1024,1]{2,1,0,3:T(8,128)} %bitcast.196, f32[4,2,8]{2,1,0:T(2,128)S(1)} %convert_reduce_fusion.1), kind=kOutput, calls=%fused_computation.56 | convolution fusion | flops 50855936 | bytes 3145984 | tf_op jit(solution)/shard_map/mcl,lrw->mcrw/dot_general | solution.py:151
  50.2 7.2 %all-to-all-done.2 = bf16[4,2,64,1024]{3,1,2,0:T(2,128)(2,1)S(1)} async-done(((bf16[4,2,64,1024]{3,1,2,0:T(2,128)(2,1)}), bf16[4,2,64,1024]{3,1,2,0:T(2,128)(2,1)S(1)}, u32[]{:S(2)}, u32[]{:S(2)}) %all-to-all-start.2) | async-done | bytes 1048608 | tf_op jit(solution)/shard_map/all_to_all | solution.py:159
  58.4 4.2 all-to-all-start.8
  64.0 13.2 %all-to-all-done.8 = bf16[4,2,64,1024]{3,1,2,0:T(2,128)(2,1)} async-done(((bf16[4,2,64,1024]{3,1,2,0:T(2,128)(2,1)}), bf16[4,2,64,1024]{3,1,2,0:T(2,128)(2,1)}, u32[]{:S(2)}, u32[]{:S(2)}) %all-to-all-start.8) | async-done | bytes 1048608 | tf_op jit(solution)/shard_map/all_to_all | solution.py:156
  77.2 6.7 %all-to-all-start.10 = ((bf16[128,8,512]{0,2,1:T(8,128)(2,1)}), bf16[128,8,512]{0,2,1:T(8,128)(2,1)S(1)}, u32[]{:S(2)}, u32[]{:S(2)}) async-start(bf16[128,8,512]{0,2,1:T(8,128)(2,1)} %bitcast.60), calls=%async_computation.10 | async-start | bytes 2097152 | tf_op jit(solution)/shard_map/all_to_all | solution.py:124
  86.3 23.2 %all-to-all-done.10 = bf16[128,8,512]{0,2,1:T(8,128)(2,1)S(1)} async-done(((bf16[128,8,512]{0,2,1:T(8,128)(2,1)}), bf16[128,8,512]{0,2,1:T(8,128)(2,1)S(1)}, u32[]{:S(2)}, u32[]{:S(2)}) %all-to-all-start.10) | async-done | bytes 1048608 | tf_op jit(solution)/shard_map/all_to_all | solution.py:124
  119.1 52.7 %all-to-all-done.3 = bf16[128,8,1024]{0,2,1:T(8,128)(2,1)S(1)} async-done(((bf16[128,8,1024]{0,2,1:T(8,128)(2,1)}), bf16[128,8,1024]{0,2,1:T(8,128)(2,1)S(1)}, u32[]{:S(2)}, u32[]{:S(2)}) %all-to-all-start.3) | async-done | bytes 2097184 | tf_op jit(solution)/shard_map/all_to_all | solution.py:123
  173.0 4.3 all-to-all-start.6
  186.2 49.0 %all-to-all-done.6 = bf16[128,8,1024]{0,2,1:T(8,128)(2,1)} async-done(((bf16[128,8,1024]{0,2,1:T(8,128)(2,1)}), bf16[128,8,1024]{0,2,1:T(8,128)(2,1)}, u32[]{:S(2)}, u32[]{:S(2)}) %all-to-all-start.6) | async-done | bytes 2097184 | tf_op jit(solution)/shard_map/all_to_all | solution.py:122
  235.1 4.4 all-to-all-start
  265.5 4.3 all-to-all-start.1
  281.1 27.9 %all-gather.9.cloned.1.call-done = bf16[8192,64]{0,1:T(8,128)(2,1)} async-done(((bf16[1024,64]{0,1:T(8,128)(2,1)}), bf16[8192,64]{0,1:T(8,128)(2,1)}) %all-gather.9.cloned.1.call-update) | async-done | bytes 1048592 | tf_op jit(solution)/shard_map/all_gather | solution.py:17
  314.6 49.0 %while.12 = (s32[]{:T(128)}, bf16[2,512,4,128]{3,2,1,0:T(4,128)(2,1)}, s32[2]{0:T(128)S(1)}, bf16[1280,4,128]{2,0,1:T(8,128)(2,1)S(1)}, s32[1024]{0:T(1024)S(1)}...) while((s32[]{:T(128)}, ...), condition=%wide.region_11.13_spmd, body=%wide.region_7.12_spmd.sunk | while | flops 1230110720 | bytes 50923260 | solution.py:99
  318.3 5.0 fusion.110
  325.1 7.5 %fusion.111 = (f32[4,512]{1,0:T(4,128)S(1)}, f32[4,512,768]{2,1,0:T(8,128)S(1)}) fusion(f32[4,512,768]{2,1,0:T(8,128)} %fusion.110, pred[512,768]{1,0:T(8,128)(4,1)S(1)} %compare_and_fusion.4), kind=kOutput, calls=%fused_computation.142.clone.1 | output fusion | flops 9437951 | bytes 12984320 | tf_op jit(solution)/shard_map/while/body/eval_jaxpr/sub | solution.py:85
  342.8 5.0 fusion.110
  349.6 7.5 %fusion.111 = (f32[4,512]{1,0:T(4,128)S(1)}, f32[4,512,768]{2,1,0:T(8,128)S(1)}) fusion(f32[4,512,768]{2,1,0:T(8,128)} %fusion.110, pred[512,768]{1,0:T(8,128)(4,1)S(1)} %compare_and_fusion.4), kind=kOutput, calls=%fused_computation.142.clone.1 | output fusion | flops 9437951 | bytes 12984320 | tf_op jit(solution)/shard_map/while/body/eval_jaxpr/sub | solution.py:85
  367.0 70.4 %all-reduce.6.cloned.1.call-done = (bf16[1024,64]{0,1:T(8,128)(2,1)}, bf16[1024,64]{0,1:T(8,128)(2,1)}, bf16[1024,64]{0,1:T(8,128)(2,1)}) async-done(((bf16[1024,64]{0,1:T(8,128)(2,1)}, bf16[1024,64]{0,1:T(8,128)(2,1)}, bf16[1024,64]{0,1:T(8,128)(2,1)}), (bf16[1024,64]{0,1:T(8,128)(2,1)}, bf16[1024,64]{0,1:T(8,128)(2,1)}, bf16[1024,64]{0,1:T(8,128)(2,1)})) %all-reduce.6.cloned.1.call-update) | async-done | bytes 393232 | tf_op jit(solution)/shard_map/psum | solution.py:219
  452.3 4.3 all-to-all-done.9
  480.2 7.4 %all-to-all-done.12 = bf16[4,2,64,1024]{3,1,2,0:T(2,128)(2,1)S(1)} async-done(((bf16[4,2,64,1024]{3,1,2,0:T(2,128)(2,1)}), bf16[4,2,64,1024]{3,1,2,0:T(2,128)(2,1)S(1)}, u32[]{:S(2)}, u32[]{:S(2)}) %all-to-all-start.12) | async-done | bytes 1048608 | tf_op jit(solution)/shard_map/all_to_all | solution.py:256
  487.6 4.4 all-to-all-start.7
  506.5 4.3 convolution_bitcast_fusion.1
  (185 shorter events, 168.7 us)
Async XLA Ops:
  7.2 23.0 %copy-start = (f32[8,64,1024]{2,1,0:T(8,128)S(1)}, f32[8,64,1024]{2,1,0:T(8,128)}, u32[]{:S(2)}) copy-start(f32[8,64,1024]{2,1,0:T(8,128)} %param.31) | copy-start | bytes 6291460
  8.7 34.3 %copy-start.26 = (f32[4,2,8]{2,1,0:T(2,128)}, f32[4,2,8]{2,1,0:T(2,128)S(1)}, u32[]{:S(2)}) copy-start(f32[4,2,8]{2,1,0:T(2,128)S(1)} %convert_reduce_fusion.1) | copy-start | bytes 772
  13.1 13.7 %all-to-all-start.4 = ((bf16[4,2,64,512]{3,1,2,0:T(2,128)(2,1)}), bf16[4,2,64,512]{3,1,2,0:T(2,128)(2,1)}, u32[]{:S(2)}, u32[]{:S(2)}) async-start(bf16[4,2,64,512]{3,1,2,0:T(2,128)(2,1)} %copy.141), calls=%async_computation.4 | async-start | bytes 1048576 | tf_op jit(solution)/shard_map/all_to_all | solution.py:158
  26.7 12.3 %all-to-all-start.5 = ((bf16[4,2,64,512]{3,2,1,0:T(8,128)(2,1)}), bf16[4,2,64,512]{3,2,1,0:T(8,128)(2,1)S(1)}, u32[]{:S(2)}, u32[]{:S(2)}) async-start(bf16[4,2,64,512]{3,2,1,0:T(8,128)(2,1)} %copy.151), calls=%async_computation.5 | async-start | bytes 1048576 | tf_op jit(solution)/shard_map/all_to_all | solution.py:157
  39.0 18.4 %all-to-all-start.2 = ((bf16[4,2,64,1024]{3,1,2,0:T(2,128)(2,1)}), bf16[4,2,64,1024]{3,1,2,0:T(2,128)(2,1)S(1)}, u32[]{:S(2)}, u32[]{:S(2)}) async-start(bf16[4,2,64,1024]{3,1,2,0:T(2,128)(2,1)} %copy.134), calls=%async_computation.2 | async-start | bytes 2097152 | tf_op jit(solution)/shard_map/all_to_all | solution.py:159
  48.4 14.3 %copy-start.12 = (bf16[1,128,4096]{2,1,0:T(8,128)(2,1)S(1)}, bf16[1,128,4096]{2,1,0:T(8,128)(2,1)}, u32[]{:S(2)}) copy-start(bf16[1,128,4096]{2,1,0:T(8,128)(2,1)} %param.20) | copy-start | bytes 3145732
  58.4 18.8 %all-to-all-start.8 = ((bf16[4,2,64,1024]{3,1,2,0:T(2,128)(2,1)}), bf16[4,2,64,1024]{3,1,2,0:T(2,128)(2,1)}, u32[]{:S(2)}, u32[]{:S(2)}) async-start(bf16[4,2,64,1024]{3,1,2,0:T(2,128)(2,1)} %copy.162), calls=%async_computation.8 | async-start | bytes 2097152 | tf_op jit(solution)/shard_map/all_to_all | solution.py:156
  62.7 21.2 %copy-start.7 = (bf16[1,128,8192]{2,1,0:T(8,128)(2,1)S(1)}, bf16[1,128,8192]{2,1,0:T(8,128)(2,1)}, u32[]{:S(2)}) copy-start(bf16[1,128,8192]{2,1,0:T(8,128)(2,1)} %param.19) | copy-start | bytes 6291460
  77.2 32.4 %all-to-all-start.10 = ((bf16[128,8,512]{0,2,1:T(8,128)(2,1)}), bf16[128,8,512]{0,2,1:T(8,128)(2,1)S(1)}, u32[]{:S(2)}, u32[]{:S(2)}) async-start(bf16[128,8,512]{0,2,1:T(8,128)(2,1)} %bitcast.60), calls=%async_computation.10 | async-start | bytes 2097152 | tf_op jit(solution)/shard_map/all_to_all | solution.py:124
  110.5 61.2 %all-to-all-start.3 = ((bf16[128,8,1024]{0,2,1:T(8,128)(2,1)}), bf16[128,8,1024]{0,2,1:T(8,128)(2,1)S(1)}, u32[]{:S(2)}, u32[]{:S(2)}) async-start(bf16[128,8,1024]{0,2,1:T(8,128)(2,1)} %bitcast.189), calls=%async_computation.3 | async-start | bytes 4194304 | tf_op jit(solution)/shard_map/all_to_all | solution.py:123
  114.2 157.2 %all-gather.7.cloned.1.call-start = ((), (), s32[]{:S(2)}) async-start(), calls=%async_computation.13 | async-start | bytes 1179648 | tf_op jit(solution)/shard_map/all_gather | solution.py:132
  173.0 62.1 %all-to-all-start.6 = ((bf16[128,8,1024]{0,2,1:T(8,128)(2,1)}), bf16[128,8,1024]{0,2,1:T(8,128)(2,1)}, u32[]{:S(2)}, u32[]{:S(2)}) async-start(bf16[128,8,1024]{0,2,1:T(8,128)(2,1)} %bitcast.188), calls=%async_computation.6 | async-start | bytes 4194304 | tf_op jit(solution)/shard_map/all_to_all | solution.py:122
  177.4 95.8 %all-gather.11.cloned.1.call-start = ((), (), s32[]{:S(2)}) async-start(), calls=%async_computation.15 | async-start | bytes 1179648 | tf_op jit(solution)/shard_map/all_gather | solution.py:133
  235.1 30.4 %all-to-all-start = ((bf16[128,8,512]{0,2,1:T(8,128)(2,1)}), bf16[128,8,512]{0,2,1:T(8,128)(2,1)}, u32[]{:S(2)}, u32[]{:S(2)}) async-start(bf16[128,8,512]{0,2,1:T(8,128)(2,1)} %bitcast.10), calls=%async_computation | async-start | bytes 2097152 | tf_op jit(solution)/shard_map/all_to_all | solution.py:126
  239.6 69.5 %all-gather.9.cloned.1.call-start = ((), (), s32[]{:S(2)}) async-start(), calls=%async_computation.14 | async-start | bytes 1179648 | tf_op jit(solution)/shard_map/all_gather | solution.py:17
  265.5 46.1 %all-to-all-start.1 = ((bf16[128,8,512]{0,2,1:T(8,128)(2,1)}), bf16[128,8,512]{0,2,1:T(8,128)(2,1)}, u32[]{:S(2)}, u32[]{:S(2)}) async-start(bf16[128,8,512]{0,2,1:T(8,128)(2,1)} %bitcast.12), calls=%async_computation.1 | async-start | bytes 2097152 | tf_op jit(solution)/shard_map/all_to_all | solution.py:125
  269.8 167.6 %all-reduce.6.cloned.1.call-start = ((), (), s32[]{:S(2)}) async-start(), calls=%async_computation.16 | async-start | bytes 786432 | tf_op jit(solution)/shard_map/psum | solution.py:219
  281.1 30.5 %copy-start.23 = (bf16[8,64,512]{2,0,1:T(8,128)(2,1)S(1)}, bf16[8,64,512]{2,0,1:T(8,128)(2,1)}, u32[]{:S(2)}) copy-start(bf16[8,64,512]{2,0,1:T(8,128)(2,1)} %copy-done.22) | copy-start | bytes 1572868
  443.5 13.1 %all-to-all-start.9 = ((bf16[4,2,64,512]{3,1,2,0:T(2,128)(2,1)}), bf16[4,2,64,512]{3,1,2,0:T(2,128)(2,1)}, u32[]{:S(2)}, u32[]{:S(2)}) async-start(bf16[4,2,64,512]{3,1,2,0:T(2,128)(2,1)} %copy.166), calls=%async_computation.9 | async-start | bytes 1048576 | tf_op jit(solution)/shard_map/all_to_all | solution.py:242
  449.6 11.1 %copy-start.10 = (bf16[8,128,1024]{2,1,0:T(8,128)(2,1)S(1)}, bf16[8,128,1024]{2,1,0:T(8,128)(2,1)}, u32[]{:S(2)}) copy-start(bf16[8,128,1024]{2,1,0:T(8,128)(2,1)} %copy.138) | copy-start | bytes 6291460
  456.6 13.1 %all-to-all-start.11 = ((bf16[4,2,64,512]{3,1,2,0:T(2,128)(2,1)}), bf16[4,2,64,512]{3,1,2,0:T(2,128)(2,1)}, u32[]{:S(2)}, u32[]{:S(2)}) async-start(bf16[4,2,64,512]{3,1,2,0:T(2,128)(2,1)} %copy.172), calls=%async_computation.11 | async-start | bytes 1048576 | tf_op jit(solution)/shard_map/all_to_all | solution.py:249
  469.6 18.0 %all-to-all-start.12 = ((bf16[4,2,64,1024]{3,1,2,0:T(2,128)(2,1)}), bf16[4,2,64,1024]{3,1,2,0:T(2,128)(2,1)S(1)}, u32[]{:S(2)}, u32[]{:S(2)}) async-start(bf16[4,2,64,1024]{3,1,2,0:T(2,128)(2,1)} %copy.177), calls=%async_computation.12 | async-start | bytes 2097152 | tf_op jit(solution)/shard_map/all_to_all | solution.py:256
  478.4 13.6 %copy-start.27 = (f32[4,2,8]{2,1,0:T(2,128)S(1)}, f32[4,2,8]{2,1,0:T(2,128)}, u32[]{:S(2)}) copy-start(f32[4,2,8]{2,1,0:T(2,128)} %copy-done.26) | copy-start | bytes 772
  487.6 18.9 %all-to-all-start.7 = ((bf16[4,2,64,1024]{3,1,2,0:T(2,128)(2,1)}), bf16[4,2,64,1024]{3,1,2,0:T(2,128)(2,1)}, u32[]{:S(2)}, u32[]{:S(2)}) async-start(bf16[4,2,64,1024]{3,1,2,0:T(2,128)(2,1)} %copy.157), calls=%async_computation.7 | async-start | bytes 2097152 | tf_op jit(solution)/shard_map/all_to_all | solution.py:235
  (23 other events, 103.2 us)
Sparse Core Ops, SparseCore 0:
  117.0 61.5 all-gather.6
  180.7 61.1 all-gather.10
  260.7 48.3 all-gather.8
  367.1 70.1 all-reduce.5
